TPU v7x, 32 devices: a whole 2x2x4 slice. The times are simulated.
32 devices in a mesh: dp: 8 (over y, x, core), tensor: 4 (over z).
Axes of the slice: x: 2, y: 2, z: 4, core: 2. Of those that a mesh axis runs over, the one named last changes fastest.
Arguments:
- activations: bfloat16 [584, 16, 1024], P('tensor', 'dp'), may hold values from -6 to 6
- cotangent: bfloat16 [584, 16, 1024], P('tensor', 'dp'), may hold values from -6 to 6
- token_valid: int32 [16, 584], P('dp'), may hold values from 0 to 1, as said below
- image_counts: int32 [8], P('dp'), may hold values from 1 to 2, as said below
- pre_gain: bfloat16 [1024], P('dp'), may hold values from 0.5 to 1.5
- pre_shift: bfloat16 [1024], P('dp'), may hold values from -3 to 3
- attn_weight: bfloat16 [3, 1024, 1024], P(None, 'dp', 'tensor'), may hold values from -0.1875 to 0.1875
- attn_bias: bfloat16 [2, 1024], P(None, 'tensor'), may hold values from -3 to 3
- proj_weight: bfloat16 [1024, 1024], P('tensor', 'dp'), may hold values from -0.5 to 0.5
- proj_bias: bfloat16 [1024], P('dp'), may hold values from -3 to 3
- mid_gain: bfloat16 [1024], P('dp'), may hold values from 0.5 to 1.5
- mid_shift: bfloat16 [1024], P('dp'), may hold values from -3 to 3
- up_weight: bfloat16 [1024, 4096], P('dp', 'tensor'), may hold values from -0.1875 to 0.1875
- up_bias: bfloat16 [4096], P('tensor'), may hold values from -3 to 3
- down_weight: bfloat16 [4096, 1024], P('tensor', 'dp'), may hold values from -0.09375 to 0.09375
- down_bias: bfloat16 [1024], P('dp'), may hold values from -3 to 3
Outputs:
- block_out: bfloat16 [584, 16, 1024], P('tensor', 'dp')
- input_grad: float32 [584, 16, 1024], P('tensor', 'dp')
- pregain_grad: float32 [1024], P('dp')
- preshift_grad: float32 [1024], P('dp')
- attnweight_grad: float32 [3, 1024, 1024], P(None, 'dp', 'tensor')
- attnbias_grad: float32 [2, 1024], P(None, 'tensor')
- projweight_grad: float32 [1024, 1024], P('tensor', 'dp')
- projbias_grad: float32 [1024], P('dp')
- midgain_grad: float32 [1024], P('dp')
- midshift_grad: float32 [1024], P('dp')
- upweight_grad: float32 [1024, 4096], P('dp', 'tensor')
- upbias_grad: float32 [4096], P('tensor')
- downweight_grad: float32 [4096, 1024], P('tensor', 'dp')
- downbias_grad: float32 [1024], P('dp')
Inputs may be any that keep to these rules, and one draw needn't show every extreme that they name: `token_valid`: the valid tokens of each image are a leading run of 292 or more positions, followed only by padding. The slots of a dp index that hold images are its first image_counts ones; in every draw some dp index holds 2 images.
All inputs are finite; a program needn't handle non-finite values.
Results may differ from a plain program's by a relative error of at most 0.012.
Values may be sent and summed in bfloat16 or wider, within the bound.
A program may use at most 192 MiB of HBM per device.

v0:
```python
import jax
import jax.numpy as jnp
from jax import lax
from jax.sharding import PartitionSpec as P

D = 1024
H = 16
HD = 64
MB = 2
EPS = 1e-06
NEG = -1000000000.0


def layer_norm(values, gain, shift):
    center = values - jnp.mean(values, axis=-1, keepdims=True)
    spread = jnp.mean(center * center, axis=-1, keepdims=True)
    return center * lax.rsqrt(spread + EPS) * gain + shift


def gelu_exact(values):
    return jax.nn.gelu(values, approximate=False)


def per_device(
    activations,
    cotangent,
    token_valid,
    image_counts,
    pre_gain,
    pre_shift,
    attn_weight,
    attn_bias,
    proj_weight,
    proj_bias,
    mid_gain,
    mid_shift,
    up_weight,
    up_bias,
    down_weight,
    down_bias,
):
    f32 = jnp.float32
    bf16 = jnp.bfloat16
    tensor_size = lax.axis_size("tensor")
    local_rows = activations.shape[0]
    slots = activations.shape[1]
    per_micro = slots // MB
    heads_here = H // tensor_size
    width_here = attn_weight.shape[2]
    hidden_here = up_weight.shape[1]
    scale = HD ** (-0.5)
    first_row = lax.axis_index("tensor") * local_rows
    my_valid = lax.dynamic_slice_in_dim(token_valid, first_row, local_rows, 1).astype(f32)
    slot_live = (jnp.arange(slots, dtype=jnp.int32) < image_counts[0]).astype(f32)
    attn_bias_f = attn_bias.astype(f32)
    up_bias_f = up_bias.astype(f32)
    acc_attn = jnp.zeros((3, D, width_here), f32)
    acc_proj = jnp.zeros((width_here, D), f32)
    acc_up = jnp.zeros((D, hidden_here), f32)
    acc_down = jnp.zeros((hidden_here, D), f32)
    acc_attn_bias = jnp.zeros((2, width_here), f32)
    acc_up_bias = jnp.zeros((hidden_here,), f32)
    acc_vectors = [jnp.zeros((D,), f32) for unused in range(6)]
    block_parts = []
    input_parts = []
    for micro_step in range(MB):
        gathered = (
            lax.all_gather(attn_weight, "dp", axis=1, tiled=True),
            lax.all_gather(proj_weight, "dp", axis=1, tiled=True),
            lax.all_gather(up_weight, "dp", axis=0, tiled=True),
            lax.all_gather(down_weight, "dp", axis=1, tiled=True),
            lax.all_gather(pre_gain, "dp", axis=0, tiled=True),
            lax.all_gather(pre_shift, "dp", axis=0, tiled=True),
            lax.all_gather(proj_bias, "dp", axis=0, tiled=True),
            lax.all_gather(mid_gain, "dp", axis=0, tiled=True),
            lax.all_gather(mid_shift, "dp", axis=0, tiled=True),
            lax.all_gather(down_bias, "dp", axis=0, tiled=True),
        )
        qkv_full, proj_full, upw_full, downw_full = (
            gathered[0],
            gathered[1],
            gathered[2],
            gathered[3],
        )
        gain_one, shift_one, proj_bias_f, gain_two, shift_two, down_bias_f = [
            item.astype(f32) for item in gathered[4:]
        ]
        offset = micro_step * per_micro
        inputs_f = activations[:, offset : offset + per_micro].astype(f32)
        key_valid = token_valid[offset : offset + per_micro]
        key_bias = jnp.where(key_valid > 0, 0.0, NEG).astype(f32)
        out_mask = jnp.transpose(
            slot_live[offset : offset + per_micro][:, None] * my_valid[offset : offset + per_micro]
        )[:, :, None]
        normed = layer_norm(inputs_f, gain_one, shift_one).astype(bf16)
        normed_all = lax.all_gather(normed, "tensor", axis=0, tiled=True)
        full_rows = normed_all.shape[0]
        projected = jnp.einsum("sid,cde->csie", normed_all, qkv_full, preferred_element_type=f32)
        queries = (
            (projected[0] + attn_bias_f[0])
            .astype(bf16)
            .reshape(full_rows, per_micro, heads_here, HD)
        )
        keys = projected[1].astype(bf16).reshape(full_rows, per_micro, heads_here, HD)
        values = (
            (projected[2] + attn_bias_f[1])
            .astype(bf16)
            .reshape(full_rows, per_micro, heads_here, HD)
        )

        def scores_of(query_part, key_part):
            raw = jnp.einsum("qihe,kihe->ihqk", query_part, key_part, preferred_element_type=f32)
            return raw * scale + key_bias[:, None, None, :]

        scores = scores_of(queries, keys)
        top = jnp.max(scores, axis=-1, keepdims=True)
        expo = jnp.exp(scores - top)
        total = jnp.sum(expo, axis=-1, keepdims=True)
        logsum = top + jnp.log(total)
        probs_low = (expo / total).astype(bf16)
        attended = (
            jnp.einsum("ihqk,kihe->qihe", probs_low, values, preferred_element_type=f32)
            .astype(bf16)
            .reshape(full_rows, per_micro, width_here)
        )
        resid = (
            inputs_f
            + lax.psum_scatter(
                jnp.einsum("sie,ed->sid", attended, proj_full, preferred_element_type=f32),
                "tensor",
                scatter_dimension=0,
                tiled=True,
            )
            + proj_bias_f
        )
        normed2 = layer_norm(resid, gain_two, shift_two).astype(bf16)
        normed2_all = lax.all_gather(normed2, "tensor", axis=0, tiled=True)
        hidden_pre = (
            jnp.einsum("sid,df->sif", normed2_all, upw_full, preferred_element_type=f32) + up_bias_f
        )
        hidden = gelu_exact(hidden_pre).astype(bf16)
        mlp_out = (
            lax.psum_scatter(
                jnp.einsum("sif,fd->sid", hidden, downw_full, preferred_element_type=f32).astype(
                    jnp.bfloat16
                ),
                "tensor",
                scatter_dimension=0,
                tiled=True,
            ).astype(jnp.float32)
            + down_bias_f
        )
        block_parts.append(((resid + mlp_out) * out_mask).astype(bf16))
        outer = cotangent[:, offset : offset + per_micro].astype(f32) * out_mask
        mlp_grad = outer.astype(bf16)
        acc_vectors[5] = acc_vectors[5] + jnp.sum(mlp_grad.astype(f32), axis=(0, 1))
        mlp_grad_all = lax.all_gather(mlp_grad, "tensor", axis=0, tiled=True)
        acc_down = acc_down + jnp.einsum(
            "sif,sid->fd", hidden, mlp_grad_all, preferred_element_type=f32
        )
        hidden_grad = jnp.einsum(
            "sid,fd->sif", mlp_grad_all, downw_full, preferred_element_type=f32
        )
        unused, gelu_back = jax.vjp(gelu_exact, hidden_pre)
        pre_grad = gelu_back(hidden_grad)[0].astype(bf16)
        acc_up_bias = acc_up_bias + jnp.sum(pre_grad.astype(f32), axis=(0, 1))
        acc_up = acc_up + jnp.einsum(
            "sid,sif->df", normed2_all, pre_grad, preferred_element_type=f32
        )
        normed2_grad = lax.psum_scatter(
            jnp.einsum("sif,df->sid", pre_grad, upw_full, preferred_element_type=f32),
            "tensor",
            scatter_dimension=0,
            tiled=True,
        )
        unused, second_back = jax.vjp(layer_norm, resid, gain_two, shift_two)
        resid_part, gain_two_grad, shift_two_grad = second_back(normed2_grad)
        acc_vectors[3] = acc_vectors[3] + gain_two_grad
        acc_vectors[4] = acc_vectors[4] + shift_two_grad
        resid_grad = outer + resid_part
        branch_grad = resid_grad.astype(bf16)
        acc_vectors[2] = acc_vectors[2] + jnp.sum(branch_grad.astype(f32), axis=(0, 1))
        branch_all = lax.all_gather(branch_grad, "tensor", axis=0, tiled=True)
        acc_proj = acc_proj + jnp.einsum(
            "sie,sid->ed", attended, branch_all, preferred_element_type=f32
        )
        att_grad = (
            jnp.einsum("sid,ed->sie", branch_all, proj_full, preferred_element_type=f32)
            .astype(bf16)
            .reshape(full_rows, per_micro, heads_here, HD)
        )
        probs = jnp.exp(scores_of(queries, keys) - logsum)
        probs_again = probs.astype(bf16)
        value_grad = jnp.einsum(
            "ihqk,qihe->kihe", probs_again, att_grad, preferred_element_type=f32
        ).astype(bf16)
        prob_grad = jnp.einsum("qihe,kihe->ihqk", att_grad, values, preferred_element_type=f32)
        score_grad = (
            probs * (prob_grad - jnp.sum(prob_grad * probs, axis=-1, keepdims=True))
        ).astype(bf16)
        query_grad = (
            jnp.einsum("ihqk,kihe->qihe", score_grad, keys, preferred_element_type=f32) * scale
        ).astype(bf16)
        key_grad = (
            jnp.einsum("ihqk,qihe->kihe", score_grad, queries, preferred_element_type=f32) * scale
        ).astype(bf16)
        qkv_grad = jnp.stack([query_grad, key_grad, value_grad]).reshape(
            3, full_rows, per_micro, width_here
        )
        acc_attn_bias = acc_attn_bias + jnp.stack(
            [
                jnp.sum(qkv_grad[0].astype(f32), axis=(0, 1)),
                jnp.sum(qkv_grad[2].astype(f32), axis=(0, 1)),
            ]
        )
        acc_attn = acc_attn + jnp.einsum(
            "sid,csie->cde", normed_all, qkv_grad, preferred_element_type=f32
        )
        normed_grad = lax.psum_scatter(
            jnp.einsum("csie,cde->sid", qkv_grad, qkv_full, preferred_element_type=f32),
            "tensor",
            scatter_dimension=0,
            tiled=True,
        )
        unused, first_back = jax.vjp(layer_norm, inputs_f, gain_one, shift_one)
        input_part, gain_one_grad, shift_one_grad = first_back(normed_grad)
        acc_vectors[0] = acc_vectors[0] + gain_one_grad
        acc_vectors[1] = acc_vectors[1] + shift_one_grad
        input_parts.append(resid_grad + input_part)
    summed = lax.psum(
        (
            acc_vectors[0],
            acc_vectors[1],
            acc_vectors[2],
            acc_vectors[3],
            acc_vectors[4],
            acc_vectors[5],
        ),
        "tensor",
    )
    owned = (
        lax.psum_scatter(acc_attn, "dp", scatter_dimension=1, tiled=True),
        lax.psum_scatter(acc_proj, "dp", scatter_dimension=1, tiled=True),
        lax.psum_scatter(acc_up, "dp", scatter_dimension=0, tiled=True),
        lax.psum_scatter(acc_down, "dp", scatter_dimension=1, tiled=True),
        lax.psum_scatter(summed[0], "dp", scatter_dimension=0, tiled=True),
        lax.psum_scatter(summed[1], "dp", scatter_dimension=0, tiled=True),
        lax.psum_scatter(summed[2], "dp", scatter_dimension=0, tiled=True),
        lax.psum_scatter(summed[3], "dp", scatter_dimension=0, tiled=True),
        lax.psum_scatter(summed[4], "dp", scatter_dimension=0, tiled=True),
        lax.psum_scatter(summed[5], "dp", scatter_dimension=0, tiled=True),
    )
    bias_sums = lax.psum((acc_attn_bias, acc_up_bias), "dp")
    block_out = jnp.concatenate(block_parts, axis=1)
    input_grad = jnp.concatenate(input_parts, axis=1)
    return (
        block_out,
        input_grad,
        owned[4],
        owned[5],
        owned[0],
        bias_sums[0],
        owned[1],
        owned[6],
        owned[7],
        owned[8],
        owned[2],
        bias_sums[1],
        owned[3],
        owned[9],
    )


def solution(mesh):
    return jax.shard_map(
        per_device,
        mesh=mesh,
        in_specs=(
            P("tensor", "dp", None),
            P("tensor", "dp", None),
            P("dp", None),
            P("dp"),
            P("dp"),
            P("dp"),
            P(None, "dp", "tensor"),
            P(None, "tensor"),
            P("tensor", "dp"),
            P("dp"),
            P("dp"),
            P("dp"),
            P("dp", "tensor"),
            P("tensor"),
            P("tensor", "dp"),
            P("dp"),
        ),
        out_specs=(
            P("tensor", "dp", None),
            P("tensor", "dp", None),
            P("dp"),
            P("dp"),
            P(None, "dp", "tensor"),
            P(None, "tensor"),
            P("tensor", "dp"),
            P("dp"),
            P("dp"),
            P("dp"),
            P("dp", "tensor"),
            P("tensor"),
            P("tensor", "dp"),
            P("dp"),
        ),
        check_vma=False,
    )
```

profile of v0, /device:TPU:0, one launch (start us, length us, event | category | flops | bytes accessed | tf_op | source)
XLA Modules:
  0.0 1428.0 jit_solution(13615151279646853309)
XLA Ops:
  7.2 3.1 convert_reduce_fusion.11
  10.4 10.3 all-gather
  20.7 8.6 all-gather.1
  29.3 5.2 multiply_reduce_fusion.13
  39.6 9.6 all_gather.68
  49.2 40.0 %all-gather.28.cloned.1.call-done = bf16[584,1,1024]{2,1,0:T(2,128)(2,1)} async-done(((bf16[146,1,1024]{2,1,0:T(2,128)(2,1)}), bf16[584,1,1024]{2,1,0:T(2,128)(2,1)}) %all-gather.28.cloned.1.call-update) | async-done | bytes 1196048 | tf_op jit(solution)/shard_map/all_gather | solution.py:96
  89.3 26.4 %all-gather.20.cloned.1.call-done = bf16[3,1024,256]{2,1,0:T(8,128)(2,1)} async-done(((bf16[3,128,256]{2,1,0:T(8,128)(2,1)}), bf16[3,1024,256]{2,1,0:T(8,128)(2,1)}) %all-gather.20.cloned.1.call-update) | async-done | bytes 1572880 | tf_op jit(solution)/shard_map/all_gather | solution.py:68
  115.7 3.3 convolution_bitcast_fusion.6
  119.1 49.8 %all-gather.18.cloned.1.call-done = bf16[584,1,1024]{2,1,0:T(2,128)(2,1)} async-done(((bf16[146,1,1024]{2,1,0:T(2,128)(2,1)}), bf16[584,1,1024]{2,1,0:T(2,128)(2,1)}) %all-gather.18.cloned.1.call-update) | async-done | bytes 1196048 | tf_op jit(solution)/shard_map/all_gather | solution.py:96
  168.9 3.3 convolution_bitcast_fusion.7
  185.2 3.9 copy.127
  194.9 3.9 copy.133
  199.5 8.7 all-gather.2
  208.3 8.7 all-gather.3
  216.9 7.8 all-gather.4
  226.0 146.3 %all-reduce.30.cloned.1.call-done = (f32[584,1,1024]{2,1,0:T(1,128)}, f32[584,1,1024]{2,1,0:T(1,128)}) async-done(((f32[584,1,1024]{2,1,0:T(1,128)}, f32[584,1,1024]{2,1,0:T(1,128)}), (f32[584,1,1024]{2,1,0:T(1,128)}, f32[584,1,1024]{2,1,0:T(1,128)})) %all-reduce.30.cloned.1.call-update) | async-done | bytes 4784144
  372.3 4.0 fusion.112
  385.8 15.3 %all-gather.24.cloned.1.call-done = bf16[1024,1024]{1,0:T(8,128)(2,1)} async-done(((bf16[128,1024]{1,0:T(8,128)(2,1)}), bf16[1024,1024]{1,0:T(8,128)(2,1)}) %all-gather.24.cloned.1.call-update) | async-done | bytes 2097168 | tf_op jit(solution)/shard_map/all_gather | solution.py:70
  401.1 52.6 %all-gather.30.cloned.1.call-done = bf16[584,1,1024]{2,1,0:T(2,128)(2,1)} async-done(((bf16[146,1,1024]{2,1,0:T(2,128)(2,1)}), bf16[584,1,1024]{2,1,0:T(2,128)(2,1)}) %all-gather.30.cloned.1.call-update) | async-done | bytes 1196048 | tf_op jit(solution)/shard_map/all_gather | solution.py:137
  453.7 5.1 fusion.57
  458.8 47.0 %all-gather.22.cloned.1.call-done = bf16[584,1,1024]{2,1,0:T(2,128)(2,1)} async-done(((bf16[146,1,1024]{2,1,0:T(2,128)(2,1)}), bf16[584,1,1024]{2,1,0:T(2,128)(2,1)}) %all-gather.22.cloned.1.call-update) | async-done | bytes 1196048 | tf_op jit(solution)/shard_map/all_gather | solution.py:137
  505.7 16.0 %multiply_convert_fusion.3 = (bf16[584,1024]{1,0:T(8,128)(2,1)}, f32[584,1024]{1,0:T(8,128)}, bf16[584,1024]{1,0:T(8,128)(2,1)}, f32[584,1024]{1,0:T(8,128)}, f32[584,1024]{1,0:T(8,128)}) fusion(f32[1024]{0:T(1024)S(1)} %convert_element_type.338, f32[584,1024]{1,0:T(8,128)} %fusion.57, bf16[1024,1024]{1,0:T(8,128)(2,1)} %all-gather.24.cloned.1.call-done, ...), kind=kOutput, calls=%fused_computation.44 | convolution fusion | flops 1303674880 | bytes 15257600 | tf_op jit(solution)/shard_map/sid,df->sif/dot_general | solution.py:139
  521.8 13.0 all-gather.26.cloned.1.call-done
  534.8 4.6 fusion.26
  539.4 2.5 fusion.27
  541.9 48.2 %fusion.106 = (bf16[152,1024]{1,0:T(8,128)(2,1)S(1)}, bf16[152,1024]{1,0:T(8,128)(2,1)}) fusion(bf16[584,1,1024]{2,0,1:T(8,128)(2,1)} %fusion.27, bf16[584,1,1024]{2,0,1:T(8,128)(2,1)} %fusion.26), kind=kCustom, calls=%all-reduce-scatter.2 | all-reduce-scatter fusion | flops 1245185 | bytes 3015168
  590.9 3.4 collective-permute-start
  595.6 8.7 all-gather.5
  606.9 3.3 concatenate.10
  612.0 2.9 concatenate.11
  615.9 8.2 multiply_convert_fusion.5
  628.0 47.2 %all-gather.32.cloned.1.call-done = bf16[584,1,1024]{2,1,0:T(2,128)(2,1)} async-done(((bf16[146,1,1024]{2,1,0:T(2,128)(2,1)}), bf16[584,1,1024]{2,1,0:T(2,128)(2,1)}) %all-gather.32.cloned.1.call-update) | async-done | bytes 1196048 | tf_op jit(solution)/shard_map/all_gather | solution.py:157
  675.2 6.1 convert_reduce_fusion.1
  683.8 3.9 copy.135
  687.6 38.9 %all-gather.36.cloned.1.call-done = bf16[584,1,1024]{2,1,0:T(2,128)(2,1)} async-done(((bf16[146,1,1024]{2,1,0:T(2,128)(2,1)}), bf16[584,1,1024]{2,1,0:T(2,128)(2,1)}) %all-gather.36.cloned.1.call-update) | async-done | bytes 1196048 | tf_op jit(solution)/shard_map/all_gather | solution.py:157
  726.5 6.1 convert_reduce_fusion
  735.1 3.8 copy.144
  739.2 173.2 %all-reduce.28.cloned.1.call-done = (f32[584,1,1024]{2,1,0:T(1,128)}, f32[584,1,1024]{2,1,0:T(1,128)}) async-done(((f32[584,1,1024]{2,1,0:T(1,128)}, f32[584,1,1024]{2,1,0:T(1,128)}), (f32[584,1,1024]{2,1,0:T(1,128)}, f32[584,1,1024]{2,1,0:T(1,128)})) %all-reduce.28.cloned.1.call-update) | async-done | bytes 4784144
  912.3 5.0 multiply_reduce_fusion.3
  917.4 6.1 fusion.109
  929.7 46.1 %all-gather.34.cloned.1.call-done = bf16[584,1,1024]{2,1,0:T(2,128)(2,1)} async-done(((bf16[146,1,1024]{2,1,0:T(2,128)(2,1)}), bf16[584,1,1024]{2,1,0:T(2,128)(2,1)}) %all-gather.34.cloned.1.call-update) | async-done | bytes 1196048 | tf_op jit(solution)/shard_map/all_gather | solution.py:183
  975.7 2.9 convolution_convert_fusion.3
  979.8 4.4 multiply_reduce_fusion.1
  990.3 37.4 %all-gather.38.cloned.1.call-done = bf16[584,1,1024]{2,1,0:T(2,128)(2,1)} async-done(((bf16[146,1,1024]{2,1,0:T(2,128)(2,1)}), bf16[584,1,1024]{2,1,0:T(2,128)(2,1)}) %all-gather.38.cloned.1.call-update) | async-done | bytes 1196048 | tf_op jit(solution)/shard_map/all_gather | solution.py:183
  1030.2 3.9 convert_reduce_fusion.2
  1034.1 4.2 multiply_reduce_fusion
  1042.4 3.8 fusion.65
  1046.2 3.3 add_bitcast_fusion
  1049.6 2.5 convolution_bitcast_fusion.2
  1052.2 3.9 copy.143
  1057.2 3.8 copy.152
  1062.4 3.7 fusion.50
  1066.1 4.0 convolution_add_fusion
  1071.4 3.8 fusion.61
  1075.2 4.0 convolution_add_fusion.1
  1087.9 6.9 reduce-scatter.11.cloned.1.call-done
  1096.7 174.9 %all-reduce.26.cloned.1.call-done = (f32[584,1,1024]{2,1,0:T(1,128)}, f32[584,1,1024]{2,1,0:T(1,128)}) async-done(((f32[584,1,1024]{2,1,0:T(1,128)}, f32[584,1,1024]{2,1,0:T(1,128)}), (f32[584,1,1024]{2,1,0:T(1,128)}, f32[584,1,1024]{2,1,0:T(1,128)})) %all-reduce.26.cloned.1.call-update) | async-done | bytes 4784144
  1271.7 5.0 multiply_reduce_fusion.5
  1276.7 25.3 %all-reduce.16 = (f32[1024]{0:T(1024)S(1)}, f32[1024]{0:T(1024)S(1)}, f32[2,256]{1,0:T(2,128)}, f32[1024]{0:T(1024)S(1)}, f32[1024]{0:T(1024)S(1)}, /*index=5*/f...) all-reduce(f32[1024]{0:T(1024)S(1)} %add.380, ...), channel_id=10, replica_groups=mesh['dp'=8,'tensor'=4] {'dp'}, use_global_device_ids=true, to_apply=%region_33.34.clone | all-reduce | flops 7680 | bytes 61440
  1302.4 10.2 all-reduce.17
  1312.7 5.4 fusion.107
  1321.6 4.2 reduce-scatter.17.cloned.1.call-done
  1325.8 55.5 %reduce-scatter.15.cloned.1.call-done = f32[128,1024]{1,0:T(8,128)} async-done(((f32[1024,1024]{1,0:T(8,128)}), f32[128,1024]{1,0:T(8,128)}) %reduce-scatter.15.cloned.1.call-update) | async-done | bytes 524304 | tf_op jit(solution)/shard_map/reduce_scatter | solution.py:244
  1381.3 39.6 %reduce-scatter.13.cloned.1.call-done = f32[256,128]{1,0:T(8,128)} async-done(((f32[256,1024]{1,0:T(8,128)}), f32[256,128]{1,0:T(8,128)}) %reduce-scatter.13.cloned.1.call-update) | async-done | bytes 131088 | tf_op jit(solution)/shard_map/reduce_scatter | solution.py:243
  (290 shorter events, 86.9 us)
Async XLA Ops:
  7.2 82.1 %all-gather.28.cloned.1.call-start = ((), (), s32[]{:S(2)}) async-start(), calls=%async_computation.9 | async-start | bytes 2990080 | tf_op jit(solution)/shard_map/all_gather | solution.py:96
  20.7 17.1 %copy-start.38 = (f32[8,1,128]{2,1,0:T(1,128)}, f32[8,1,128]{2,1,0:T(1,128)S(1)}, u32[]{:S(2)}) copy-start(f32[8,1,128]{2,1,0:T(1,128)S(1)} %convert_element_type.404) | copy-start | bytes 12292
  34.5 84.5 %copy-start.48 = (f32[146]{0:T(256)}, f32[146]{0:T(256)S(1)}, u32[]{:S(2)}) copy-start(f32[146]{0:T(256)S(1)} %get-tuple-element.152) | copy-start | bytes 1756
  34.5 4.8 copy-start.52
  34.5 5.0 copy-start.45
  34.6 5.0 copy-start.40
  37.8 77.9 %all-gather.20.cloned.1.call-start = ((), (), s32[]{:S(2)}) async-start(), calls=%async_computation.5 | async-start | bytes 1769472 | tf_op jit(solution)/shard_map/all_gather | solution.py:68
  38.5 130.4 %all-gather.18.cloned.1.call-start = ((), (), s32[]{:S(2)}) async-start(), calls=%async_computation.4 | async-start | bytes 2990080 | tf_op jit(solution)/shard_map/all_gather | solution.py:96
  39.3 333.0 %all-reduce.30.cloned.1.call-start = ((), (), s32[]{:S(2)}) async-start(), calls=%async_computation.21 | async-start | bytes 9568256
  49.2 145.2 %copy-start.15 = (bf16[256,1024]{1,0:T(8,128)(2,1)}, bf16[256,1024]{1,0:T(8,128)(2,1)S(1)}, u32[]{:S(2)}) copy-start(bf16[256,1024]{1,0:T(8,128)(2,1)S(1)} %all_gather.68) | copy-start | bytes 1572868
  174.5 17.1 %copy-start.19 = (f32[1,584,1,256]{1,3,2,0:T(8,128)}, f32[1,584,1,256]{1,3,2,0:T(8,128)S(1)}, u32[]{:S(2)}) copy-start(f32[1,584,1,256]{1,3,2,0:T(8,128)S(1)} %copy.129) | copy-start | bytes 1794052
  175.9 5.0 copy-start.17
  184.7 4.4 copy-start.25
  194.4 4.5 copy-start.27
  198.8 9.4 copy-start.54
  198.8 18.1 %copy-start.55 = (bf16[128]{0:T(256)(128)(2,1)S(1)}, bf16[128]{0:T(256)(128)(2,1)}, u32[]{:S(2)}) copy-start(bf16[128]{0:T(256)(128)(2,1)} %param.27) | copy-start | bytes 772
  198.8 25.9 %copy-start.51 = (u32[32]{0:T(128)S(1)}, u32[32]{0:T(128)}, u32[]{:S(2)}) copy-start(u32[32]{0:T(128)} %constant.109) | copy-start | bytes 388
  198.8 173.4 %copy-start.2 = (bf16[146,2,1024]{2,1,0:T(2,128)(2,1)S(1)}, bf16[146,2,1024]{2,1,0:T(2,128)(2,1)}, u32[]{:S(2)}) copy-start(bf16[146,2,1024]{2,1,0:T(2,128)(2,1)} %param.16) | copy-start | bytes 1794052
  198.9 202.2 %all-gather.24.cloned.1.call-start = ((), (), s32[]{:S(2)}) async-start(), calls=%async_computation.7 | async-start | bytes 2359296 | tf_op jit(solution)/shard_map/all_gather | solution.py:70
  199.5 254.2 %all-gather.30.cloned.1.call-start = ((), (), s32[]{:S(2)}) async-start(), calls=%async_computation.10 | async-start | bytes 2990080 | tf_op jit(solution)/shard_map/all_gather | solution.py:137
  376.3 6.4 copy-start.13
  376.3 6.4 copy-start.14
  378.3 7.4 copy-start.50
  382.7 123.1 %all-gather.22.cloned.1.call-start = ((), (), s32[]{:S(2)}) async-start(), calls=%async_computation.6 | async-start | bytes 2990080 | tf_op jit(solution)/shard_map/all_gather | solution.py:137
  383.4 151.4 %all-gather.26.cloned.1.call-start = ((), (), s32[]{:S(2)}) async-start(), calls=%async_computation.8 | async-start | bytes 2359296 | tf_op jit(solution)/shard_map/all_gather | solution.py:71
  384.2 291.0 %all-gather.32.cloned.1.call-start = ((), (), s32[]{:S(2)}) async-start(), calls=%async_computation.11 | async-start | bytes 2990080 | tf_op jit(solution)/shard_map/all_gather | solution.py:157
  534.8 4.6 copy-start.30
  534.8 4.6 copy-start.59
  541.9 53.6 %copy-start.56 = (bf16[128]{0:T(256)(128)(2,1)S(1)}, bf16[128]{0:T(256)(128)(2,1)}, u32[]{:S(2)}) copy-start(bf16[128]{0:T(256)(128)(2,1)} %param.31) | copy-start | bytes 772
  590.9 16.0 %collective-permute-start = (bf16[18,1024]{1,0:T(8,128)(2,1)S(1)}, bf16[18,1024]{1,0:T(8,128)(2,1)S(1)}, u32[]{:S(2)}, u32[]{:S(2)}) collective-permute-start(bf16[18,1024]{1,0:T(8,128)(2,1)S(1)} %slice.94), channel_id=1, source_target_pairs={{0,1},{1,2},{2,3},{4,5},{5,6},{6,7},{8,9},{9,10},{10,11},{12,13},{... | collective-permute-start | bytes 110600
  605.0 7.0 collective-permute-start.1
  624.1 57.2 %copy-start.9 = (f32[146,1,1024]{2,1,0:T(1,128)}, f32[146,1,1024]{2,1,0:T(1,128)S(1)}, u32[]{:S(2)}) copy-start(f32[146,1,1024]{2,1,0:T(1,128)S(1)} %get-tuple-element.173) | copy-start | bytes 1794052
  626.2 100.4 %all-gather.36.cloned.1.call-start = ((), (), s32[]{:S(2)}) async-start(), calls=%async_computation.13 | async-start | bytes 2990080 | tf_op jit(solution)/shard_map/all_gather | solution.py:157
  627.5 284.9 %all-reduce.28.cloned.1.call-start = ((), (), s32[]{:S(2)}) async-start(), calls=%async_computation.20 | async-start | bytes 9568256
  675.2 7.2 copy-start.57
  726.5 7.1 copy-start.58
  738.9 236.8 %all-gather.34.cloned.1.call-start = ((), (), s32[]{:S(2)}) async-start(), calls=%async_computation.12 | async-start | bytes 2990080 | tf_op jit(solution)/shard_map/all_gather | solution.py:183
  917.3 6.1 copy-start.12
  925.5 50.2 %copy-start.16 = (bf16[256,1024]{1,0:T(8,128)(2,1)S(1)}, bf16[256,1024]{1,0:T(8,128)(2,1)}, u32[]{:S(2)}) copy-start(bf16[256,1024]{1,0:T(8,128)(2,1)} %copy-done.15) | copy-start | bytes 1572868
  925.5 102.2 %all-gather.38.cloned.1.call-start = ((), (), s32[]{:S(2)}) async-start(), calls=%async_computation.14 | async-start | bytes 2990080 | tf_op jit(solution)/shard_map/all_gather | solution.py:183
  929.6 165.2 %reduce-scatter.11.cloned.1.call-start = ((), (), s32[]{:S(2)}) async-start(), calls=%async_computation.15 | async-start | bytes 3538944 | tf_op jit(solution)/shard_map/reduce_scatter | solution.py:242
  979.8 4.5 slice-start.2
  979.8 5.0 slice-start.3
  1030.1 4.0 copy-start.20
  1030.1 8.2 slice-start
  1034.1 4.2 slice-start.1
  1042.4 3.8 copy-start.34
  1049.6 222.0 %all-reduce.26.cloned.1.call-start = ((), (), s32[]{:S(2)}) async-start(), calls=%async_computation.19 | async-start | bytes 9568256
  1052.2 3.9 copy-start.60
  1061.1 5.0 copy-start.31
  1061.1 264.7 %reduce-scatter.17.cloned.1.call-start = ((), (), s32[]{:S(2)}) async-start(), calls=%async_computation.18 | async-start | bytes 4718592 | tf_op jit(solution)/shard_map/reduce_scatter | solution.py:245
  1070.1 5.1 copy-start.33
  1070.1 311.2 %reduce-scatter.15.cloned.1.call-start = ((), (), s32[]{:S(2)}) async-start(), calls=%async_computation.17 | async-start | bytes 4718592 | tf_op jit(solution)/shard_map/reduce_scatter | solution.py:244
  1079.3 4.4 copy-start.26
  1079.3 6.9 copy-start.28
  1079.3 341.6 %reduce-scatter.13.cloned.1.call-start = ((), (), s32[]{:S(2)}) async-start(), calls=%async_computation.16 | async-start | bytes 1179648 | tf_op jit(solution)/shard_map/reduce_scatter | solution.py:243
  1086.2 185.4 %copy-start.4 = (f32[146,1,1024]{2,1,0:T(1,128)S(1)}, f32[146,1,1024]{2,1,0:T(1,128)}, u32[]{:S(2)}) copy-start(f32[146,1,1024]{2,1,0:T(1,128)} %copy-done.3) | copy-start | bytes 1794052
  1086.2 185.4 %copy-start.6 = (f32[146,1,1024]{2,1,0:T(1,128)S(1)}, f32[146,1,1024]{2,1,0:T(1,128)}, u32[]{:S(2)}) copy-start(f32[146,1,1024]{2,1,0:T(1,128)} %copy-done.5) | copy-start | bytes 1794052
  1086.2 185.4 %copy-start.39 = (f32[8,1,128]{2,1,0:T(1,128)S(1)}, f32[8,1,128]{2,1,0:T(1,128)}, u32[]{:S(2)}) copy-start(f32[8,1,128]{2,1,0:T(1,128)} %copy-done.38) | copy-start | bytes 12292
  1086.2 185.4 %copy-start.42 = (f32[146]{0:T(256)S(1)}, f32[146]{0:T(256)}, u32[]{:S(2)}) copy-start(f32[146]{0:T(256)} %copy-done.41) | copy-start | bytes 1756
  1086.2 185.4 %copy-start.44 = (f32[146]{0:T(256)S(1)}, f32[146]{0:T(256)}, u32[]{:S(2)}) copy-start(f32[146]{0:T(256)} %copy-done.43) | copy-start | bytes 1756
  1087.9 188.8 %copy-start.49 = (f32[146]{0:T(256)S(1)}, f32[146]{0:T(256)}, u32[]{:S(2)}) copy-start(f32[146]{0:T(256)} %copy-done.48) | copy-start | bytes 1756
  1087.9 188.8 %copy-start.47 = (f32[146]{0:T(256)S(1)}, f32[146]{0:T(256)}, u32[]{:S(2)}) copy-start(f32[146]{0:T(256)} %copy-done.46) | copy-start | bytes 1756
  1312.7 6.1 copy-start.8
  (25 other events, 45.0 us)
Sparse Core Ops, SparseCore 0:
  37.9 51.3 all-gather.27
  91.2 24.4 all-gather.19
  117.8 51.0 all-gather.17
  199.0 173.2 all-reduce.29
  374.2 26.8 all-gather.23
  402.6 51.0 all-gather.29
  455.9 49.8 all-gather.21
  507.8 26.9 all-gather.25
  626.3 48.8 all-gather.31
  676.6 49.8 all-gather.35
  739.1 173.2 all-reduce.27
  925.7 50.0 all-gather.33
  977.8 49.8 all-gather.37
  1049.7 45.0 reduce-scatter.10
  1097.2 174.4 all-reduce.25
  1275.4 50.3 reduce-scatter.16
  1329.9 51.3 reduce-scatter.14
  1384.9 35.9 reduce-scatter.12
where the time goes:
time: 1430 us
  waiting for transfers between devices  1020 us (71%)
  blocking collectives  146 us (10%)
  matrix products  110 us (8%)
  other arithmetic  69.8 us (5%)
  local copies, waits for them, and re-layouts  58.6 us (4%)
  between operations  18.3 us (1%)
    unnamed x23, waiting for transfers between devices  498 us
    all_gather x2, waiting for transfers between devices, per_device(): normed2_all = lax.all_gather(normed2, 'tensor', axis=0, tiled=True)  99.5 us
    all_gather x2, waiting for transfers between devices, per_device(): normed_all = lax.all_gather(normed, 'tensor', axis=0, tiled=True)  89.8 us
    all_gather x2, waiting for transfers between devices, per_device(): mlp_grad_all = lax.all_gather(mlp_grad, 'tensor', axis=0, tiled=True)  86.1 us
    all_gather x2, waiting for transfers between devices, per_device(): branch_all = lax.all_gather(branch_grad, 'tensor', axis=0, tiled=True)  83.5 us
    unnamed x2, blocking collectives  73.4 us
    reduce_scatter x1, waiting for transfers between devices, per_device(): lax.psum_scatter(acc_up, 'dp', scatter_dimension=0, tiled=True)  55.5 us
    reduce_scatter x1, waiting for transfers between devices, per_device(): lax.psum_scatter(acc_proj, 'dp', scatter_dimension=1, tiled=True)  39.6 us
  transfers between devices with their start and end apart: 20, of which 18 were waited for; matrix products, arithmetic and copies ran while one was open for 9% of the time, Pallas kernels for 0%

commit v1 on v0

--- a/solution.py
+++ b/solution.py
@@ -154,7 +154,16 @@
         outer = cotangent[:, offset : offset + per_micro].astype(f32) * out_mask
         mlp_grad = outer.astype(bf16)
         acc_vectors[5] = acc_vectors[5] + jnp.sum(mlp_grad.astype(f32), axis=(0, 1))
-        mlp_grad_all = lax.all_gather(mlp_grad, "tensor", axis=0, tiled=True)
+        ring = [mlp_grad]
+        for hop in range(3):
+            ring.append(
+                lax.ppermute(ring[-1], "tensor", [(dev, (dev + 1) % 4) for dev in range(4)])
+            )
+        mlp_grad_all = jnp.roll(
+            jnp.concatenate(ring[::-1], axis=0),
+            (lax.axis_index("tensor") + 1) * ring[0].shape[0],
+            axis=0,
+        )
         acc_down = acc_down + jnp.einsum(
             "sif,sid->fd", hidden, mlp_grad_all, preferred_element_type=f32
         )

time: 1430 us -> 1300 us (0.909)
  waiting for transfers between devices: 1020 us -> 837 us
  blocking collectives: 146 us -> 186 us
  other arithmetic: 69.8 us -> 44.5 us
  local copies, waits for them, and re-layouts: 58.6 us -> 83.6 us
    unnamed x23 -> x21, waiting for transfers between devices: 498 us -> 403 us
    all_gather x2 -> x0, waiting for transfers between devices: 86.1 us -> none  [per_device(): mlp_grad_all = lax.all_gather(mlp_grad, 'tensor', axis=0, tiled=True)]
    unnamed x2, blocking collectives: 73.4 us -> 113 us
    ppermute x0 -> x6, waiting for transfers between devices: none -> 32.9 us  [per_device(): lax.ppermute(ring[-1], 'tensor', [(dev, (dev + 1) % 4) for dev in range(4)])]
    reduce_sum x4, other arithmetic: 18.6 us -> 2.56 us  [layer_norm(): center = values - jnp.mean(values, axis=-1, keepdims=True)]
    all_gather x1, waiting for transfers between devices: 15.3 us -> 0.01 us  [per_device(): lax.all_gather(up_weight, 'dp', axis=0, tiled=True)]
    another operation x0 -> x2, other arithmetic: none -> 14.9 us
    unnamed x153 -> x215, local copies, waits for them, and re-layouts: 24.6 us -> 30.2 us
  transfers between devices with their start and end apart: 20 -> 24, of which waited for: 18 -> 19; matrix products, arithmetic and copies ran while one was open for 9% -> 17% of each run, Pallas kernels for 0% -> 0%
where the time goes in v1:
time: 1300 us
  waiting for transfers between devices  837 us (64%)
  blocking collectives  186 us (14%)
  matrix products  108 us (8%)
  local copies, waits for them, and re-layouts  83.6 us (6%)
  other arithmetic  44.5 us (3%)
  starting transfers between devices  20 us (2%)
  between operations  18.4 us (1%)
    unnamed x21, waiting for transfers between devices  403 us
    unnamed x2, blocking collectives  113 us
    all_gather x2, waiting for transfers between devices, per_device(): normed_all = lax.all_gather(normed, 'tensor', axis=0, tiled=True)  89.5 us
    all_gather x2, waiting for transfers between devices, per_device(): normed2_all = lax.all_gather(normed2, 'tensor', axis=0, tiled=True)  86.9 us
    all_gather x2, waiting for transfers between devices, per_device(): branch_all = lax.all_gather(branch_grad, 'tensor', axis=0, tiled=True)  85.1 us
    reduce_scatter x1, waiting for transfers between devices, per_device(): lax.psum_scatter(acc_up, 'dp', scatter_dimension=0, tiled=True)  55.5 us
    reduce_scatter x1, waiting for transfers between devices, per_device(): lax.psum_scatter(acc_proj, 'dp', scatter_dimension=1, tiled=True)  39.6 us
    ppermute x6, waiting for transfers between devices, per_device(): lax.ppermute(ring[-1], 'tensor', [(dev, (dev + 1) % 4) for dev in range(4)])  32.9 us
  transfers between devices with their start and end apart: 24, of which 19 were waited for; matrix products, arithmetic and copies ran while one was open for 17% of the time, Pallas kernels for 0%

profile of v1, /device:TPU:0, one launch (start us, length us, event | category | flops | bytes accessed | tf_op | source)
XLA Modules:
  0.0 1297.6 jit_solution(15186347081766615230)
XLA Ops:
  7.2 10.3 all-gather
  17.5 8.6 all-gather.1
  33.8 9.3 all_gather.62
  43.1 39.7 %all-gather.26.cloned.1.call-done = bf16[584,1,1024]{2,1,0:T(2,128)(2,1)} async-done(((bf16[146,1,1024]{2,1,0:T(2,128)(2,1)}), bf16[584,1,1024]{2,1,0:T(2,128)(2,1)}) %all-gather.26.cloned.1.call-update) | async-done | bytes 1196048 | tf_op jit(solution)/shard_map/all_gather | solution.py:96
  82.8 26.4 %all-gather.18.cloned.1.call-done = bf16[3,1024,256]{2,1,0:T(8,128)(2,1)} async-done(((bf16[3,128,256]{2,1,0:T(8,128)(2,1)}), bf16[3,1024,256]{2,1,0:T(8,128)(2,1)}) %all-gather.18.cloned.1.call-update) | async-done | bytes 1572880 | tf_op jit(solution)/shard_map/all_gather | solution.py:68
  109.3 3.3 convolution_bitcast_fusion.6
  112.7 49.8 %all-gather.16.cloned.1.call-done = bf16[584,1,1024]{2,1,0:T(2,128)(2,1)} async-done(((bf16[146,1,1024]{2,1,0:T(2,128)(2,1)}), bf16[584,1,1024]{2,1,0:T(2,128)(2,1)}) %all-gather.16.cloned.1.call-update) | async-done | bytes 1196048 | tf_op jit(solution)/shard_map/all_gather | solution.py:96
  162.5 3.3 convolution_bitcast_fusion.7
  180.6 3.9 copy.129
  190.9 3.9 copy.138
  196.2 8.7 all-gather.2
  204.9 8.7 all-gather.3
  213.6 7.8 all-gather.4
  222.6 145.7 %all-reduce.30.cloned.1.call-done = (f32[584,1,1024]{2,1,0:T(1,128)}, f32[584,1,1024]{2,1,0:T(1,128)}) async-done(((f32[584,1,1024]{2,1,0:T(1,128)}, f32[584,1,1024]{2,1,0:T(1,128)}), (f32[584,1,1024]{2,1,0:T(1,128)}, f32[584,1,1024]{2,1,0:T(1,128)})) %all-reduce.30.cloned.1.call-update) | async-done | bytes 4784144
  384.7 8.7 collective-permute-done.3
  395.7 4.3 collective-permute-done
  400.1 6.7 collective-permute-done.4
  406.8 6.7 collective-permute-done.1
  413.6 6.5 collective-permute-done.5
  420.1 7.0 fusion.44
  427.1 7.9 fusion.52
  435.0 5.1 fusion.153
  440.1 39.9 %all-gather.28.cloned.1.call-done = bf16[584,1,1024]{2,1,0:T(2,128)(2,1)} async-done(((bf16[146,1,1024]{2,1,0:T(2,128)(2,1)}), bf16[584,1,1024]{2,1,0:T(2,128)(2,1)}) %all-gather.28.cloned.1.call-update) | async-done | bytes 1196048 | tf_op jit(solution)/shard_map/all_gather | solution.py:137
  480.0 5.1 fusion.62
  485.1 47.0 %all-gather.20.cloned.1.call-done = bf16[584,1,1024]{2,1,0:T(2,128)(2,1)} async-done(((bf16[146,1,1024]{2,1,0:T(2,128)(2,1)}), bf16[584,1,1024]{2,1,0:T(2,128)(2,1)}) %all-gather.20.cloned.1.call-update) | async-done | bytes 1196048 | tf_op jit(solution)/shard_map/all_gather | solution.py:137
  532.1 3.9 fusion.68
  536.8 15.7 %convert_reduce_fusion.1 = (f32[1024]{0:T(1024)}, bf16[584,1024]{1,0:T(8,128)(2,1)S(1)}, f32[584,1024]{1,0:T(8,128)}, f32[1024]{0:T(1024)}, bf16[584,1024]{1,0:T(8,128)(2,1)S(1)}, /*index=5*/f32[584,1024]{1,0:T(8,128)}) fusion(f32[584,1024]{1,0:T(8,128)S(1)} %fusion.68, f32[1024]{0:T(1024)S(1)} %convert_element_type.338, f32[584,1024]{1,0:T(8,128)S(1)} %copy-done.94, ...), kind=kOutput, calls=%fused_computation.44 | convolution fusion | flops 1314437120 | bytes 17657856 | tf_op jit(solution)/shard_map/sid,fd->sif/dot_general | solution.py:170
  555.0 3.9 copy.142
  560.3 3.9 copy.155
  564.3 5.2 multiply_convert_fusion.3
  569.5 2.4 fusion.26
  572.0 2.4 fusion.27
  574.4 88.4 %fusion.128 = (bf16[152,1024]{1,0:T(8,128)(2,1)}, bf16[152,1024]{1,0:T(8,128)(2,1)}) fusion(bf16[584,1,1024]{2,0,1:T(8,128)(2,1)} %fusion.27, bf16[584,1,1024]{2,0,1:T(8,128)(2,1)} %fusion.26), kind=kCustom, calls=%all-reduce-scatter.2 | all-reduce-scatter fusion | flops 1245185 | bytes 3015168
  664.2 12.2 collective-permute-start.6
  677.8 4.4 collective-permute-start.7
  682.2 8.9 all-gather.5
  692.4 3.3 concatenate.24
  695.7 3.4 concatenate.25
  699.0 80.2 %all-reduce.28.cloned.1.call-done = (f32[584,1,1024]{2,1,0:T(1,128)}, f32[584,1,1024]{2,1,0:T(1,128)}) async-done(((f32[584,1,1024]{2,1,0:T(1,128)}, f32[584,1,1024]{2,1,0:T(1,128)}), (f32[584,1,1024]{2,1,0:T(1,128)}, f32[584,1,1024]{2,1,0:T(1,128)})) %all-reduce.28.cloned.1.call-update) | async-done | bytes 4784144
  779.2 2.6 fusion.133
  789.3 48.3 %all-gather.30.cloned.1.call-done = bf16[584,1,1024]{2,1,0:T(2,128)(2,1)} async-done(((bf16[146,1,1024]{2,1,0:T(2,128)(2,1)}), bf16[584,1,1024]{2,1,0:T(2,128)(2,1)}) %all-gather.30.cloned.1.call-update) | async-done | bytes 1196048 | tf_op jit(solution)/shard_map/all_gather | solution.py:192
  837.7 2.9 convolution_convert_fusion.3
  841.8 4.4 multiply_reduce_fusion.1
  852.9 36.8 %all-gather.32.cloned.1.call-done = bf16[584,1,1024]{2,1,0:T(2,128)(2,1)} async-done(((bf16[146,1,1024]{2,1,0:T(2,128)(2,1)}), bf16[584,1,1024]{2,1,0:T(2,128)(2,1)}) %all-gather.32.cloned.1.call-update) | async-done | bytes 1196048 | tf_op jit(solution)/shard_map/all_gather | solution.py:192
  889.7 2.9 convolution_convert_fusion.2
  893.8 4.6 convert_reduce_fusion.4
  898.4 4.2 multiply_reduce_fusion
  911.9 3.9 fusion.70
  915.8 3.2 add_bitcast_fusion
  920.1 2.6 convolution_bitcast_fusion.2
  922.7 3.9 copy.152
  927.8 3.9 copy.165
  932.1 3.6 fusion.154
  935.7 3.9 convolution_add_fusion
  939.7 4.1 fusion.66
  943.9 4.1 convolution_add_fusion.1
  951.8 2.4 fusion.58
  955.9 8.3 reduce-scatter.11.cloned.1.call-done
  966.1 175.1 %all-reduce.26.cloned.1.call-done = (f32[584,1,1024]{2,1,0:T(1,128)}, f32[584,1,1024]{2,1,0:T(1,128)}) async-done(((f32[584,1,1024]{2,1,0:T(1,128)}, f32[584,1,1024]{2,1,0:T(1,128)}), (f32[584,1,1024]{2,1,0:T(1,128)}, f32[584,1,1024]{2,1,0:T(1,128)})) %all-reduce.26.cloned.1.call-update) | async-done | bytes 4784144
  1147.3 24.8 %all-reduce.16 = (f32[1024]{0:T(1024)S(1)}, f32[1024]{0:T(1024)S(1)}, f32[2,256]{1,0:T(2,128)}, f32[1024]{0:T(1024)S(1)}, f32[1024]{0:T(1024)S(1)}, /*index=5*/f...) all-reduce(f32[1024]{0:T(1024)S(1)} %add.393, ...), channel_id=10, replica_groups=mesh['dp'=8,'tensor'=4] {'dp'}, use_global_device_ids=true, to_apply=%region_33.35.clone | all-reduce | flops 7680 | bytes 61440
  1175.3 10.2 all-reduce.17
  1185.5 9.9 reduce-scatter.17.cloned.1.call-done
  1195.4 55.5 %reduce-scatter.15.cloned.1.call-done = f32[128,1024]{1,0:T(8,128)} async-done(((f32[1024,1024]{1,0:T(8,128)}), f32[128,1024]{1,0:T(8,128)}) %reduce-scatter.15.cloned.1.call-update) | async-done | bytes 524304 | tf_op jit(solution)/shard_map/reduce_scatter | solution.py:253
  1250.9 39.6 %reduce-scatter.13.cloned.1.call-done = f32[256,128]{1,0:T(8,128)} async-done(((f32[256,1024]{1,0:T(8,128)}), f32[256,128]{1,0:T(8,128)}) %reduce-scatter.13.cloned.1.call-update) | async-done | bytes 131088 | tf_op jit(solution)/shard_map/reduce_scatter | solution.py:252
  (372 shorter events, 100.8 us)
Async XLA Ops:
  7.2 75.7 %all-gather.26.cloned.1.call-start = ((), (), s32[]{:S(2)}) async-start(), calls=%async_computation.9 | async-start | bytes 2990080 | tf_op jit(solution)/shard_map/all_gather | solution.py:96
  17.5 12.2 copy-start.47
  28.6 4.8 copy-start.52
  28.9 4.5 copy-start.62
  29.7 13.4 %copy-start.72 = (f32[146]{0:T(256)}, f32[146]{0:T(256)S(1)}, u32[]{:S(2)}) copy-start(f32[146]{0:T(256)S(1)} %fusion.94) | copy-start | bytes 1756
  29.7 13.4 %copy-start.60 = (f32[146]{0:T(256)}, f32[146]{0:T(256)S(1)}, u32[]{:S(2)}) copy-start(f32[146]{0:T(256)S(1)} %fusion.120) | copy-start | bytes 1756
  31.4 77.9 %all-gather.18.cloned.1.call-start = ((), (), s32[]{:S(2)}) async-start(), calls=%async_computation.5 | async-start | bytes 1769472 | tf_op jit(solution)/shard_map/all_gather | solution.py:68
  32.1 130.4 %all-gather.16.cloned.1.call-start = ((), (), s32[]{:S(2)}) async-start(), calls=%async_computation.4 | async-start | bytes 2990080 | tf_op jit(solution)/shard_map/all_gather | solution.py:96
  33.5 334.8 %all-reduce.30.cloned.1.call-start = ((), (), s32[]{:S(2)}) async-start(), calls=%async_computation.19 | async-start | bytes 9568256
  33.7 153.5 %copy-start.58 = (f32[4,64]{1,0:T(4,128)}, f32[4,64]{1,0:T(4,128)S(1)}, u32[]{:S(2)}) copy-start(f32[4,64]{1,0:T(4,128)S(1)} %add.351) | copy-start | bytes 3076
  43.1 146.6 %copy-start.13 = (bf16[256,1024]{1,0:T(8,128)(2,1)}, bf16[256,1024]{1,0:T(8,128)(2,1)S(1)}, u32[]{:S(2)}) copy-start(bf16[256,1024]{1,0:T(8,128)(2,1)S(1)} %all_gather.62) | copy-start | bytes 1572868
  169.1 15.3 %copy-start.4 = (f32[1,584,1,256]{1,3,2,0:T(8,128)}, f32[1,584,1,256]{1,3,2,0:T(8,128)S(1)}, u32[]{:S(2)}) copy-start(f32[1,584,1,256]{1,3,2,0:T(8,128)S(1)} %copy.135) | copy-start | bytes 1794052
  170.5 5.0 copy-start.15
  194.9 10.0 copy-start.86
  194.9 18.7 %copy-start.87 = (bf16[128]{0:T(256)(128)(2,1)S(1)}, bf16[128]{0:T(256)(128)(2,1)}, u32[]{:S(2)}) copy-start(bf16[128]{0:T(256)(128)(2,1)} %param.29) | copy-start | bytes 772
  194.9 26.5 %copy-start.83 = (u32[32]{0:T(128)S(1)}, u32[32]{0:T(128)}, u32[]{:S(2)}) copy-start(u32[32]{0:T(128)} %constant.125) | copy-start | bytes 388
  194.9 240.1 %all-gather.24.cloned.1.call-start = ((), (), s32[]{:S(2)}) async-start(), calls=%async_computation.8 | async-start | bytes 2359296 | tf_op jit(solution)/shard_map/all_gather | solution.py:71
  195.5 244.5 %all-gather.22.cloned.1.call-start = ((), (), s32[]{:S(2)}) async-start(), calls=%async_computation.7 | async-start | bytes 2359296 | tf_op jit(solution)/shard_map/all_gather | solution.py:70
  196.1 283.9 %all-gather.28.cloned.1.call-start = ((), (), s32[]{:S(2)}) async-start(), calls=%async_computation.10 | async-start | bytes 2990080 | tf_op jit(solution)/shard_map/all_gather | solution.py:137
  372.4 7.4 copy-start.78
  372.4 7.4 copy-start.68
  374.7 157.4 %all-gather.20.cloned.1.call-start = ((), (), s32[]{:S(2)}) async-start(), calls=%async_computation.6 | async-start | bytes 2990080 | tf_op jit(solution)/shard_map/all_gather | solution.py:137
  377.4 18.3 %copy-start.54 = (f32[1,146]{1,0:T(1,128)}, f32[1,146]{1,0:T(1,128)S(1)}, u32[]{:S(2)}) copy-start(f32[1,146]{1,0:T(1,128)S(1)} %get-tuple-element.170) | copy-start | bytes 1756
  377.4 18.3 %copy-start.56 = (f32[1,146]{1,0:T(1,128)}, f32[1,146]{1,0:T(1,128)S(1)}, u32[]{:S(2)}) copy-start(f32[1,146]{1,0:T(1,128)S(1)} %get-tuple-element.169) | copy-start | bytes 1756
  377.4 29.4 %copy-start.82 = (bf16[1024]{0:T(1024)(128)(2,1)S(1)}, bf16[1024]{0:T(1024)(128)(2,1)}, u32[]{:S(2)}) copy-start(bf16[1024]{0:T(1024)(128)(2,1)} %param.31) | copy-start | bytes 6148
  381.3 12.2 collective-permute-start.3
  382.7 17.3 %collective-permute-start = (bf16[146,1,1024]{2,0,1:T(8,128)(2,1)}, bf16[146,1,1024]{2,0,1:T(8,128)(2,1)}, u32[]{:S(2)}, u32[]{:S(2)}) collective-permute-start(bf16[146,1,1024]{2,0,1:T(8,128)(2,1)} %get-tuple-element.111), channel_id=1, source_target_pairs={{0,1},{1,2},{2,3},{3,0},{4,5},{5,6},{6,7},{7,4},{8,9},{9,10},{10,1... | collective-permute-start | bytes 897032 | tf_op jit(solution)/shard_map/ppermute | solution.py:160
  393.4 13.3 %collective-permute-start.4 = (bf16[146,1,1024]{2,0,1:T(8,128)(2,1)}, bf16[146,1,1024]{2,0,1:T(8,128)(2,1)}, u32[]{:S(2)}, u32[]{:S(2)}) collective-permute-start(bf16[146,1,1024]{2,0,1:T(8,128)(2,1)} %collective-permute-done.3), channel_id=1, source_target_pairs={{0,1},{1,2},{2,3},{3,0},{4,5},{5,6},{6,7},{7,4},{8,9},{9,10},{10,1... | collective-permute-start | bytes 897032 | tf_op jit(solution)/shard_map/ppermute | solution.py:160
  395.7 383.5 %all-reduce.28.cloned.1.call-start = ((), (), s32[]{:S(2)}) async-start(), calls=%async_computation.18 | async-start | bytes 9568256
  400.1 13.3 %collective-permute-start.1 = (bf16[146,1,1024]{2,0,1:T(8,128)(2,1)}, bf16[146,1,1024]{2,0,1:T(8,128)(2,1)}, u32[]{:S(2)}, u32[]{:S(2)}) collective-permute-start(bf16[146,1,1024]{2,0,1:T(8,128)(2,1)} %collective-permute-done), channel_id=1, source_target_pairs={{0,1},{1,2},{2,3},{3,0},{4,5},{5,6},{6,7},{7,4},{8,9},{9,10},{10,1... | collective-permute-start | bytes 897032 | tf_op jit(solution)/shard_map/ppermute | solution.py:160
  406.8 13.3 %collective-permute-start.5 = (bf16[146,1,1024]{2,0,1:T(8,128)(2,1)}, bf16[146,1,1024]{2,0,1:T(8,128)(2,1)}, u32[]{:S(2)}, u32[]{:S(2)}) collective-permute-start(bf16[146,1,1024]{2,0,1:T(8,128)(2,1)} %collective-permute-done.4), channel_id=1, source_target_pairs={{0,1},{1,2},{2,3},{3,0},{4,5},{5,6},{6,7},{7,4},{8,9},{9,10},{10,1... | collective-permute-start | bytes 897032 | tf_op jit(solution)/shard_map/ppermute | solution.py:160
  413.4 13.7 %collective-permute-start.2 = (bf16[146,1,1024]{2,0,1:T(8,128)(2,1)}, bf16[146,1,1024]{2,0,1:T(8,128)(2,1)S(1)}, u32[]{:S(2)}, u32[]{:S(2)}) collective-permute-start(bf16[146,1,1024]{2,0,1:T(8,128)(2,1)} %collective-permute-done.1), channel_id=1, source_target_pairs={{0,1},{1,2},{2,3},{3,0},{4,5},{5,6},{6,7},{7,4},{8,9},{9,10},{10,1... | collective-permute-start | bytes 897032 | tf_op jit(solution)/shard_map/ppermute | solution.py:160
  532.1 4.7 copy-start.94
  536.8 15.7 %copy-start.22 = (f32[584,1024]{1,0:T(8,128)}, f32[584,1024]{1,0:T(8,128)S(1)}, u32[]{:S(2)}) copy-start(f32[584,1024]{1,0:T(8,128)S(1)} %fusion.68) | copy-start | bytes 7176196
  536.8 16.7 %copy-start.90 = (bf16[1024,1024]{1,0:T(8,128)(2,1)S(1)}, bf16[1024,1024]{1,0:T(8,128)(2,1)}, u32[]{:S(2)}) copy-start(bf16[1024,1024]{1,0:T(8,128)(2,1)} %all-gather.22.cloned.1.call-done) | copy-start | bytes 6291460
  552.5 6.4 copy-start.39
  564.2 273.5 %all-gather.30.cloned.1.call-start = ((), (), s32[]{:S(2)}) async-start(), calls=%async_computation.11 | async-start | bytes 2990080 | tf_op jit(solution)/shard_map/all_gather | solution.py:192
  564.2 5.3 copy-start.89
  664.2 28.2 %collective-permute-start.6 = (bf16[18,1024]{1,0:T(8,128)(2,1)}, bf16[18,1024]{1,0:T(8,128)(2,1)S(1)}, u32[]{:S(2)}, u32[]{:S(2)}) collective-permute-start(bf16[18,1024]{1,0:T(8,128)(2,1)} %slice.94), channel_id=1, source_target_pairs={{0,1},{1,2},{2,3},{4,5},{5,6},{6,7},{8,9},{9,10},{10,11},{12,13},{... | collective-permute-start | bytes 110600
  677.8 17.8 %collective-permute-start.7 = (bf16[18,1024]{1,0:T(8,128)(2,1)}, bf16[18,1024]{1,0:T(8,128)(2,1)S(1)}, u32[]{:S(2)}, u32[]{:S(2)}) collective-permute-start(bf16[18,1024]{1,0:T(8,128)(2,1)} %slice.95), channel_id=1, source_target_pairs={{0,1},{1,2},{2,3},{4,5},{5,6},{6,7},{8,9},{9,10},{10,11},{12,13},{... | collective-permute-start | bytes 110600
  786.2 51.5 %copy-start.14 = (bf16[256,1024]{1,0:T(8,128)(2,1)S(1)}, bf16[256,1024]{1,0:T(8,128)(2,1)}, u32[]{:S(2)}) copy-start(bf16[256,1024]{1,0:T(8,128)(2,1)} %copy-done.13) | copy-start | bytes 1572868
  787.5 102.2 %all-gather.32.cloned.1.call-start = ((), (), s32[]{:S(2)}) async-start(), calls=%async_computation.12 | async-start | bytes 2990080 | tf_op jit(solution)/shard_map/all_gather | solution.py:192
  787.8 54.0 %copy-start.59 = (f32[4,64]{1,0:T(4,128)S(1)}, f32[4,64]{1,0:T(4,128)}, u32[]{:S(2)}) copy-start(f32[4,64]{1,0:T(4,128)} %copy-done.58) | copy-start | bytes 3076
  789.1 175.1 %reduce-scatter.11.cloned.1.call-start = ((), (), s32[]{:S(2)}) async-start(), calls=%async_computation.13 | async-start | bytes 3538944 | tf_op jit(solution)/shard_map/reduce_scatter | solution.py:251
  841.8 4.5 slice-start.2
  841.8 5.0 slice-start.3
  893.8 4.6 copy-start.18
  893.8 8.8 slice-start
  905.6 5.0 copy-start.23
  907.0 4.5 copy-start.31
  907.0 4.7 copy-start.26
  919.1 222.2 %all-reduce.26.cloned.1.call-start = ((), (), s32[]{:S(2)}) async-start(), calls=%async_computation.17 | async-start | bytes 9568256
  931.8 263.6 %reduce-scatter.17.cloned.1.call-start = ((), (), s32[]{:S(2)}) async-start(), calls=%async_computation.16 | async-start | bytes 4718592 | tf_op jit(solution)/shard_map/reduce_scatter | solution.py:254
  939.7 311.2 %reduce-scatter.15.cloned.1.call-start = ((), (), s32[]{:S(2)}) async-start(), calls=%async_computation.15 | async-start | bytes 4718592 | tf_op jit(solution)/shard_map/reduce_scatter | solution.py:253
  948.0 342.5 %reduce-scatter.13.cloned.1.call-start = ((), (), s32[]{:S(2)}) async-start(), calls=%async_computation.14 | async-start | bytes 1179648 | tf_op jit(solution)/shard_map/reduce_scatter | solution.py:252
  955.9 188.9 %copy-start.48 = (f32[8,1,128]{2,1,0:T(1,128)S(1)}, f32[8,1,128]{2,1,0:T(1,128)}, u32[]{:S(2)}) copy-start(f32[8,1,128]{2,1,0:T(1,128)} %copy-done.47) | copy-start | bytes 12292
  955.9 188.9 %copy-start.53 = (f32[146]{0:T(256)S(1)}, f32[146]{0:T(256)}, u32[]{:S(2)}) copy-start(f32[146]{0:T(256)} %copy-done.52) | copy-start | bytes 1756
  955.9 189.2 %copy-start.75 = (f32[146]{0:T(256)S(1)}, f32[146]{0:T(256)}, u32[]{:S(2)}) copy-start(f32[146]{0:T(256)} %copy-done.74) | copy-start | bytes 1756
  955.9 189.2 %copy-start.51 = (f32[146]{0:T(256)S(1)}, f32[146]{0:T(256)}, u32[]{:S(2)}) copy-start(f32[146]{0:T(256)} %copy-done.50) | copy-start | bytes 1756
  955.9 189.2 %copy-start.63 = (f32[146]{0:T(256)S(1)}, f32[146]{0:T(256)}, u32[]{:S(2)}) copy-start(f32[146]{0:T(256)} %copy-done.62) | copy-start | bytes 1756
  1141.2 4.5 copy-start.73
  1141.2 4.5 copy-start.9
  1141.2 4.5 copy-start.61
  1145.2 27.4 %copy-start.11 = (f32[146,1,1024]{2,0,1:T(8,128)S(1)}, f32[146,1,1024]{2,0,1:T(8,128)}, u32[]{:S(2)}) copy-start(f32[146,1,1024]{2,0,1:T(8,128)} %get-tuple-element.133) | copy-start | bytes 1794052
  (59 other events, 159.2 us)
Sparse Core Ops, SparseCore 0:
  31.5 51.3 all-gather.25
  84.7 24.4 all-gather.17
  111.4 51.0 all-gather.15
  195.0 173.2 all-reduce.29
  370.2 27.1 all-gather.23
  399.3 27.8 all-gather.21
  428.9 51.0 all-gather.27
  482.2 49.8 all-gather.19
  564.3 214.8 all-reduce.27
  787.6 50.0 all-gather.29
  839.8 49.8 all-gather.31
  919.2 44.9 reduce-scatter.10
  966.8 174.4 all-reduce.25
  1145.0 50.2 reduce-scatter.16
  1199.5 51.3 reduce-scatter.14
  1254.5 35.9 reduce-scatter.12
